TPU v7x, 512 devices: a whole 4x4x16 slice. The times are simulated.
512 devices in a mesh: row: 16 (over z_hi, x, core), col: 32 (over z_lo, y).
Axes of the slice: x: 4, y: 4, z: 16 (z_hi: 2, z_lo: 8; z = z_hi * 8 + z_lo), core: 2. Of those that a mesh axis runs over, the one named last changes fastest.
Arguments:
- a_blocks: bfloat16 [384, 4096, 128], P('row', 'col'), may hold values from -6 to 6
- a_ids: int32 [16, 768], P('row', 'col'), may hold values from 0 to 31, as said below
- a_count: int32 [16, 32], P('row', 'col'), may hold values from 12 to 24, as said below
- b_blocks: bfloat16 [768, 4096, 128], P('row', 'col'), may hold values from -0.125 to 0.125
- b_ids: int32 [16, 1536], P('row', 'col'), may hold values from 0 to 31, as said below
- b_count: int32 [16, 64], P('row', 'col'), may hold values from 12 to 24, as said below
Outputs:
- product: bfloat16 [16384, 32768], P('row', 'col')
Inputs may be any that keep to these rules, and one draw needn't show every extreme that they name: `a_ids`: within each panel the 24 slots name distinct blocks; slots from a_count on are padding. `a_count`: some panel has all 24 slots occupied. `b_ids`: within each panel the 24 slots name distinct blocks; slots from b_count on are padding. `b_count`: some panel has all 24 slots occupied.
All inputs are finite; a program needn't handle non-finite values.
Results may differ from a plain program's by a relative error of at most 0.001.
Values may be sent and summed in bfloat16 or wider, within the bound.
A program may use at most 64 MiB of HBM per device.

v0:
```python
import jax
import jax.numpy as jnp
from jax import lax
from jax.sharding import PartitionSpec as P

BR = 8
BK = 4
BC = 8
TICKS = 4


def passed_along(value, axis, steps):
    count = lax.axis_size(axis)
    pairs = [(source, (source + steps) % count) for source in range(count)]
    return lax.ppermute(value, axis, pairs)


def expand(blocks, ids, count, rows, cols):
    slots = blocks.shape[0]
    width = blocks.shape[1]
    live = jnp.arange(slots, dtype=jnp.int32) < count
    numbers = jnp.arange(rows * cols, dtype=jnp.int32)
    onehot = ((ids[None, :] == numbers[:, None]) & live[None, :]).astype(jnp.bfloat16)
    dense = jnp.dot(
        onehot, blocks.reshape(slots, width * width), preferred_element_type=jnp.float32
    ).astype(jnp.bfloat16)
    return (
        dense.reshape(rows, cols, width, width)
        .transpose(0, 2, 1, 3)
        .reshape(rows * width, cols * width)
    )


def shards(a_blocks, a_ids, a_count, b_blocks, b_ids, b_count):
    width = a_blocks.shape[1]
    ratio = lax.axis_size("col") // lax.axis_size("row")
    row_count = lax.axis_size("row")
    my_row = lax.axis_index("row")
    b_slots = b_blocks.shape[0] // ratio
    total = jnp.zeros((BR * width, BC * width), jnp.float32)
    left_start = expand(a_blocks, a_ids[0], a_count[0, 0], BR, BK)
    right_start = jnp.stack(
        [
            expand(
                b_blocks[h * b_slots : (h + 1) * b_slots],
                b_ids[0, h * b_slots : (h + 1) * b_slots],
                b_count[0, h],
                BK,
                BC,
            )
            for h in range(ratio)
        ]
    )
    left, right = (left_start, right_start)
    for tick in range(TICKS):
        if tick > 0:
            left_from = left
            right_from = right
            stride = -1
            left = passed_along(left_from, "col", stride)
            right = passed_along(right_from, "row", stride)
        half = (my_row + tick) // row_count % ratio
        chosen = lax.dynamic_index_in_dim(right, half, 0, keepdims=False)
        total = total + jnp.dot(left, chosen, preferred_element_type=jnp.float32)
    return total.astype(jnp.bfloat16)


def solution(mesh):
    return jax.shard_map(
        shards,
        mesh=mesh,
        in_specs=(
            P("row", "col", None),
            P("row", "col"),
            P("row", "col"),
            P("row", "col", None),
            P("row", "col"),
            P("row", "col"),
        ),
        out_specs=P("row", "col"),
        check_vma=False,
    )
```

profile of v0, /device:TPU:248, one launch (start us, length us, event | category | flops | bytes accessed | tf_op | source)
XLA Modules:
  0.0 386.4 jit_solution(5321393752465646990)
XLA Ops:
  0.0 0.8 slice_bitcast_fusion
  0.8 1.3 fusion.37
  2.1 0.6 iota_compare_fusion.3
  2.8 0.6 iota_compare_fusion.4
  3.4 1.5 fusion.36
  4.9 0.7 fusion.1
  5.6 0.5 stack_reshape.6
  6.1 0.7 fusion.2
  7.5 10.0 %collective-permute-start.1 = (bf16[2,512,1024]{2,1,0:T(8,128)(2,1)S(1)}, bf16[2,512,1024]{2,1,0:T(8,128)(2,1)}, u32[]{:S(2)}, u32[]{:S(2)}) collective-permute-start(bf16[2,512,1024]{2,1,0:T(8,128)(2,1)S(1)} %constant_dynamic-update-slice_fusion), channel_id=1, source_target_pairs={{0,480},{32,0},{64,32},{96,64},{128,96},{160,128},{192,160},{224,1... | collective-permute-start | bytes 6291464 | tf_op jit(solution)/shard_map/ppermute | solution.py:15
  17.5 80.8 %collective-permute-done.1 = bf16[2,512,1024]{2,1,0:T(8,128)(2,1)} collective-permute-done((bf16[2,512,1024]{2,1,0:T(8,128)(2,1)S(1)}, bf16[2,512,1024]{2,1,0:T(8,128)(2,1)}, u32[]{:S(2)}, u32[]{:S(2)}) %collective-permute-start.1) | collective-permute-done | bytes 2097184 | tf_op jit(solution)/shard_map/ppermute | solution.py:15
  98.3 15.0 %collective-permute-start.3 = (bf16[2,512,1024]{2,1,0:T(8,128)(2,1)}, bf16[2,512,1024]{2,1,0:T(8,128)(2,1)}, u32[]{:S(2)}, u32[]{:S(2)}) collective-permute-start(bf16[2,512,1024]{2,1,0:T(8,128)(2,1)} %collective-permute-done.1), channel_id=1, source_target_pairs={{0,480},{32,0},{64,32},{96,64},{128,96},{160,128},{192,160},{224,1... | collective-permute-start | bytes 6291464 | tf_op jit(solution)/shard_map/ppermute | solution.py:15
  114.0 0.7 fusion
  114.9 0.7 copy.7
  115.9 2.8 collective-permute-start
  118.7 192.9 %collective-permute-done = bf16[1024,512]{0,1:T(8,128)(2,1)} collective-permute-done((bf16[1024,512]{0,1:T(8,128)(2,1)S(1)}, bf16[1024,512]{0,1:T(8,128)(2,1)}, u32[]{:S(2)}, u32[]{:S(2)}) %collective-permute-start) | collective-permute-done | bytes 1048608 | tf_op jit(solution)/shard_map/ppermute | solution.py:15
  311.6 1.9 collective-permute-start.2
  313.5 1.9 collective-permute-start.5
  315.6 29.1 %collective-permute-done.2 = bf16[1024,512]{0,1:T(8,128)(2,1)} collective-permute-done((bf16[1024,512]{0,1:T(8,128)(2,1)}, bf16[1024,512]{0,1:T(8,128)(2,1)}, u32[]{:S(2)}, u32[]{:S(2)}) %collective-permute-start.2) | collective-permute-done | bytes 1048608 | tf_op jit(solution)/shard_map/ppermute | solution.py:15
  344.7 1.9 collective-permute-start.4
  346.6 1.3 fusion.8
  347.9 2.8 fusion.6
  350.8 2.8 fusion.4
  353.6 28.6 %collective-permute-done.4 = bf16[1024,512]{0,1:T(8,128)(2,1)S(1)} collective-permute-done((bf16[1024,512]{0,1:T(8,128)(2,1)}, bf16[1024,512]{0,1:T(8,128)(2,1)S(1)}, u32[]{:S(2)}, u32[]{:S(2)}) %collective-permute-start.4) | collective-permute-done | bytes 1048608 | tf_op jit(solution)/shard_map/ppermute | solution.py:15
  382.2 4.2 %add_convert_fusion = bf16[1024,1024]{1,0:T(8,128)(2,1)} fusion(f32[1024,1024]{1,0:T(8,128)S(1)} %fusion.4, f32[1024,1024]{1,0:T(8,128)S(1)} %fusion.8, f32[1024,1024]{1,0:T(8,128)S(1)} %fusion.6, bf16[1024,512]{0,1:T(8,128)(2,1)S(1)} %collective-permute-done.4, bf16[2,512,1024]{2,1,0:T(8,128)(2,1)} %collective-permute-done.5, s32[]{:T(128)S(6)} %select_n.56), kind=kOutput, calls=%fused_computation.3 | convolution fusion | flops 1077936128 | bytes 16777220 | tf_op jit(solution)/shard_map/dot_general | solution.py:64
  (16 shorter events, 1.2 us)
Async XLA Ops:
  7.3 106.7 %copy-start.2 = (bf16[24,128,128]{2,1,0:T(8,128)(2,1)S(1)}, bf16[24,128,128]{2,1,0:T(8,128)(2,1)}, u32[]{:S(2)}) copy-start(bf16[24,128,128]{2,1,0:T(8,128)(2,1)} %param.6) | copy-start | bytes 2359300
  7.3 106.7 %copy-start.3 = (s32[1,24]{1,0:T(1,128)S(1)}, s32[1,24]{1,0:T(1,128)}, u32[]{:S(2)}) copy-start(s32[1,24]{1,0:T(1,128)} %param.7) | copy-start | bytes 292
  7.5 106.5 %copy-start = (bf16[2,512,1024]{2,1,0:T(8,128)(2,1)}, bf16[2,512,1024]{2,1,0:T(8,128)(2,1)S(1)}, u32[]{:S(2)}) copy-start(bf16[2,512,1024]{2,1,0:T(8,128)(2,1)S(1)} %constant_dynamic-update-slice_fusion) | copy-start | bytes 6291460
  7.5 90.8 %collective-permute-start.1 = (bf16[2,512,1024]{2,1,0:T(8,128)(2,1)S(1)}, bf16[2,512,1024]{2,1,0:T(8,128)(2,1)}, u32[]{:S(2)}, u32[]{:S(2)}) collective-permute-start(bf16[2,512,1024]{2,1,0:T(8,128)(2,1)S(1)} %constant_dynamic-update-slice_fusion), channel_id=1, source_target_pairs={{0,480},{32,0},{64,32},{96,64},{128,96},{160,128},{192,160},{224,1... | collective-permute-start | bytes 6291464 | tf_op jit(solution)/shard_map/ppermute | solution.py:15
  98.3 215.2 %collective-permute-start.3 = (bf16[2,512,1024]{2,1,0:T(8,128)(2,1)}, bf16[2,512,1024]{2,1,0:T(8,128)(2,1)}, u32[]{:S(2)}, u32[]{:S(2)}) collective-permute-start(bf16[2,512,1024]{2,1,0:T(8,128)(2,1)} %collective-permute-done.1), channel_id=1, source_target_pairs={{0,480},{32,0},{64,32},{96,64},{128,96},{160,128},{192,160},{224,1... | collective-permute-start | bytes 6291464 | tf_op jit(solution)/shard_map/ppermute | solution.py:15
  115.7 231.0 %copy-start.1 = (bf16[2,512,1024]{2,1,0:T(8,128)(2,1)S(1)}, bf16[2,512,1024]{2,1,0:T(8,128)(2,1)}, u32[]{:S(2)}) copy-start(bf16[2,512,1024]{2,1,0:T(8,128)(2,1)} %copy-done) | copy-start | bytes 6291460
  115.9 195.7 %collective-permute-start = (bf16[1024,512]{0,1:T(8,128)(2,1)S(1)}, bf16[1024,512]{0,1:T(8,128)(2,1)}, u32[]{:S(2)}, u32[]{:S(2)}) collective-permute-start(bf16[1024,512]{0,1:T(8,128)(2,1)S(1)} %bitcast.66), channel_id=1, source_target_pairs={{0,31},{1,0},{2,1},{3,2},{4,3},{5,4},{6,5},{7,6},{8,7},{9,8},{10,9... | collective-permute-start | bytes 3145736 | tf_op jit(solution)/shard_map/ppermute | solution.py:15
  311.6 33.1 %collective-permute-start.2 = (bf16[1024,512]{0,1:T(8,128)(2,1)}, bf16[1024,512]{0,1:T(8,128)(2,1)}, u32[]{:S(2)}, u32[]{:S(2)}) collective-permute-start(bf16[1024,512]{0,1:T(8,128)(2,1)} %collective-permute-done), channel_id=1, source_target_pairs={{0,31},{1,0},{2,1},{3,2},{4,3},{5,4},{6,5},{7,6},{8,7},{9,8},{10,9... | collective-permute-start | bytes 3145736 | tf_op jit(solution)/shard_map/ppermute | solution.py:15
  313.5 68.6 %collective-permute-start.5 = (bf16[2,512,1024]{2,1,0:T(8,128)(2,1)}, bf16[2,512,1024]{2,1,0:T(8,128)(2,1)}, u32[]{:S(2)}, u32[]{:S(2)}) collective-permute-start(bf16[2,512,1024]{2,1,0:T(8,128)(2,1)} %collective-permute-done.3), channel_id=1, source_target_pairs={{0,480},{32,0},{64,32},{96,64},{128,96},{160,128},{192,160},{224,1... | collective-permute-start | bytes 6291464 | tf_op jit(solution)/shard_map/ppermute | solution.py:15
  344.7 37.5 %collective-permute-start.4 = (bf16[1024,512]{0,1:T(8,128)(2,1)}, bf16[1024,512]{0,1:T(8,128)(2,1)S(1)}, u32[]{:S(2)}, u32[]{:S(2)}) collective-permute-start(bf16[1024,512]{0,1:T(8,128)(2,1)} %collective-permute-done.2), channel_id=1, source_target_pairs={{0,31},{1,0},{2,1},{3,2},{4,3},{5,4},{6,5},{7,6},{8,7},{9,8},{10,9... | collective-permute-start | bytes 3145736 | tf_op jit(solution)/shard_map/ppermute | solution.py:15
where the time goes:
time: 387 us; the launch traced here: 386 us
  waiting for transfers between devices  331 us (86%)
  starting transfers between devices  33.5 us (9%)
  matrix products  13.2 us (3%)
  local copies, waits for them, and re-layouts  5.99 us (2%)
    ppermute x6, waiting for transfers between devices, passed_along(): return lax.ppermute(value, axis, pairs)  331 us
    ppermute x6, starting transfers between devices, passed_along(): return lax.ppermute(value, axis, pairs)  33.5 us
    dot_general x4, matrix products, shards(): total = total + jnp.dot(left, chosen, preferred_element_type=jnp.float32)  11.2 us
  transfers between devices with their start and end apart: 6, of which 4 were waited for; matrix products, arithmetic and copies ran while one was open for 2% of the time, Pallas kernels for 0%

commit v1 on v0

v1 whole, which is shorter than its diff:
```python
import functools

import jax
import jax.numpy as jnp
from jax import lax
from jax.experimental import pallas as pl
from jax.experimental.pallas import tpu as pltpu
from jax.sharding import PartitionSpec as P

BR = 8
BK = 4
BC = 8
TICKS = 4
LANES = 8
MESH = pl.DeviceIdType.MESH


def exchange(
    n_row, n_col, a, b, ma, mb, ra, rb, ra_meta, rb_meta,
    lane_in, lane_mid, lane_out, sem_a, sem_b, sem_m, sem_l, send_sems,
):
    i, j = lax.axis_index("row"), lax.axis_index("col")
    n_zlo = n_col // 4
    n_z = n_row // LANES * n_zlo
    hop = n_z // 4
    zh, lane = i // LANES, i % LANES
    x, core = lane // 2, lane % 2
    zl, y = j // 4, j % 4
    z = zh * n_zlo + zl
    slots = a.shape[0]
    pieces = 4
    part = slots // pieces
    share = slots // LANES

    def along_z(steps):
        there = (z + steps + n_z) % n_z
        return ((there // n_zlo) * LANES + lane, (there % n_zlo) * 4 + y)

    barrier = pltpu.get_barrier_semaphore()
    away = hop * (1 - 2 * core)
    senders = [(zh * LANES + (lane + d) % LANES, j) for d in range(1, LANES)]
    senders += [((i + t) % n_row, j) for t in range(1, TICKS)]
    senders += [(i, (j + t) % n_col) for t in range(1, TICKS + 1)]
    senders += [(i, zl * 4 + (y + 1) % 4), (i, zl * 4 + (y + 3) % 4)]
    senders += [along_z(-away)]
    for sender in senders:
        pl.semaphore_signal(barrier, inc=1, device_id=sender, device_id_type=MESH)
    pl.semaphore_wait(barrier, len(senders))

    pending = []

    def send(src, dst, sem, device, slot=None):
        slot = len(pending) if slot is None else slot
        return pltpu.make_async_remote_copy(
            src_ref=src, dst_ref=dst, send_sem=send_sems.at[slot], recv_sem=sem,
            device_id=device, device_id_type=MESH,
        )

    def start(cond, make):
        slot = len(pending)
        pending.append((cond, functools.partial(make, slot)))
        if cond is None:
            make(slot).start()
        else:
            pl.when(cond)(lambda: make(slot).start())

    def arrived(ref, sem):
        pltpu.make_async_copy(ref, ref, sem).wait()

    def pa(slot, k):
        return ra.at[slot, pl.ds(k * part, part)]

    def pb(slot, k):
        return rb.at[slot, pl.ds(k * part, part)]

    for t in range(1, TICKS):
        start(None, lambda s, t=t: send(ma, ra_meta.at[t - 1], sem_m.at[t - 1], (i, (j - t + n_col) % n_col), s))
        start(None, lambda s, t=t: send(mb, rb_meta.at[t - 1], sem_m.at[t + 2], ((i - t + n_row) % n_row, j), s))

    base = slots * (1 - zh)

    @pl.when(lane < 3)
    def _():
        pltpu.make_async_copy(
            b.at[pl.ds(base + share * lane, share)], lane_in.at[lane], sem_l.at[0, lane]
        ).start()

    for d in range(1, LANES):
        to = (lane + d) % LANES
        start(
            lane < 3,
            lambda s, to=to: send(
                b.at[pl.ds(base + share * to, share)], lane_in.at[lane], sem_l.at[0, lane], (zh * LANES + to, j), s
            ),
        )

    up = (y + 2) // 3
    far = (i, (zl - 1 + y // 3 + n_zlo) % n_zlo * 4 + (y + up) % 4)
    far_slot = 3 - up
    for k in range(pieces):
        mine = a.at[pl.ds(k * part, part)]
        start(None, lambda s, k=k, mine=mine: send(mine, pa(far_slot, k), sem_a.at[far_slot, k], far, s))
        start(y > 0, lambda s, k=k, mine=mine: send(mine, pa(0, k), sem_a.at[0, k], (i, j - 1), s))
        own = b.at[pl.ds(k * part, part)]
        start(x > 0, lambda s, k=k, own=own: send(own, pb(1, k), sem_b.at[1, k], (i - 2, j), s))
        start(core == 1, lambda s, k=k, own=own: send(own, pb(0, k), sem_b.at[0, k], (i - 1, j), s))

    def lanes_first(p):
        arrived(lane_in.at[p], sem_l.at[0, p])
        start(None, lambda s: send(lane_in.at[p], lane_mid.at[p], sem_l.at[1, p], along_z(away), s))

    def lanes_second(p):
        arrived(lane_mid.at[p], sem_l.at[1, p])
        start(None, lambda s: send(lane_mid.at[p], lane_out.at[p], sem_l.at[2, p], along_z(away), s))

    def lanes_last(p):
        arrived(lane_out.at[p], sem_l.at[2, p])
        goal = 6 if p == 0 else 7
        slot = 2 if p == 2 else 1
        into = rb.at[slot, pl.ds(lane * share, share)]
        sem = sem_b.at[slot, lane // 2]

        @pl.when(lane == goal)
        def _():
            pltpu.make_async_copy(lane_out.at[p], into, sem).start()

        start(lane != goal, lambda s: send(lane_out.at[p], into, sem, (zh * LANES + goal, j), s))

    def near(to):
        return (i, zl * 4 + to)

    def forward_first(k):
        low = k < pieces // 2

        @pl.when(y == 0)
        def _():
            arrived(pa(3, k), sem_a.at[3, k])

        start(y == 0, lambda s: send(pa(3, k), pa(2, k), sem_a.at[2, k], near(1), s))
        start(y == 0, lambda s: send(pa(3, k), pa(0, k), sem_a.at[0, k], near(3), s))

        @pl.when((y == 1) | (y == 2))
        def _():
            arrived(pa(0, k), sem_a.at[0, k])

        start(y == 1, lambda s: send(pa(0, k), pa(1, k), sem_a.at[1, k], near(0), s))
        if not low:
            start(y == 2, lambda s: send(pa(0, k), pa(1, k), sem_a.at[1, k], near(1), s))

        @pl.when((y == 0) | (y == 2))
        def _():
            arrived(pa(2, k), sem_a.at[2, k])

        start(y == 2, lambda s: send(pa(2, k), pa(1, k), sem_a.at[1, k], near(3), s))
        if low:
            start(y == 0, lambda s: send(pa(2, k), pa(1, k), sem_a.at[1, k], near(1), s))

    def forward_second(k):
        low = k < pieces // 2

        @pl.when(y == 1)
        def _():
            arrived(pa(2, k), sem_a.at[2, k])

        @pl.when(y == 3)
        def _():
            arrived(pa(0, k), sem_a.at[0, k])

        if low:
            start(y == 1, lambda s: send(pa(2, k), pa(1, k), sem_a.at[1, k], near(2), s))
        else:
            start(y == 3, lambda s: send(pa(0, k), pa(1, k), sem_a.at[1, k], near(2), s))

    def forward_b(k, here):
        @pl.when(here)
        def _():
            arrived(pb(1, k), sem_b.at[1, k])

        start(here & (core == 0), lambda s: send(pb(1, k), pb(0, k), sem_b.at[0, k], (i + 1, j), s))
        start(here & (lane > 0), lambda s: send(pb(1, k), pb(2, k), sem_b.at[2, k], (i - 1, j), s))

    for p in range(3):
        lanes_first(p)
    for k in range(pieces):
        forward_first(k)
        forward_b(k, x < 3)
        forward_second(k)
        if k > 0:
            lanes_second(k - 1)
    for p in range(3):
        lanes_last(p)
    for k in range(pieces):
        forward_b(k, x == 3)

    for k in range(pieces):
        arrived(pa(1, k), sem_a.at[1, k])

        @pl.when(y == 0)
        def _():
            arrived(pa(0, k), sem_a.at[0, k])

        @pl.when(y == 3)
        def _():
            arrived(pa(2, k), sem_a.at[2, k])

        arrived(pb(0, k), sem_b.at[0, k])
        arrived(pb(2, k), sem_b.at[2, k])
    for t in range(TICKS - 1):
        arrived(ra_meta.at[t], sem_m.at[t])
        arrived(rb_meta.at[t], sem_m.at[t + 3])
    for cond, make in pending:
        if cond is None:
            make().wait_send()
        else:
            pl.when(cond)(lambda make=make: make().wait_send())


def gather_panels(n_row, n_col, a, b, ma, mb):
    block = a.shape[1:]
    slots = a.shape[0]
    share = slots // LANES
    hbm = pl.BlockSpec(memory_space=pl.ANY)
    return pl.pallas_call(
        functools.partial(exchange, n_row, n_col),
        out_shape=[
            jax.ShapeDtypeStruct((TICKS, slots) + block, a.dtype),
            jax.ShapeDtypeStruct((TICKS - 1, slots) + block, a.dtype),
            jax.ShapeDtypeStruct((TICKS - 1,) + ma.shape, jnp.int32),
            jax.ShapeDtypeStruct((TICKS - 1,) + mb.shape, jnp.int32),
        ],
        in_specs=[hbm] * 4,
        out_specs=[hbm] * 4,
        scratch_shapes=[pltpu.VMEM((3, share) + block, a.dtype)] * 3
        + [
            pltpu.SemaphoreType.DMA((4, 4)),
            pltpu.SemaphoreType.DMA((3, 4)),
            pltpu.SemaphoreType.DMA((6,)),
            pltpu.SemaphoreType.DMA((3, 3)),
            pltpu.SemaphoreType.DMA((96,)),
        ],
        compiler_params=pltpu.CompilerParams(collective_id=0, has_side_effects=True),
    )(a, b, ma, mb)


def fill(dense, at, blocks, place, rows, cols, along_rows):
    width = blocks.shape[-1]
    for number in range(rows * cols):
        r, c = number // cols, number % cols
        slot = place(number)
        block = blocks[jnp.maximum(slot - 1, 0)]
        block = jnp.where(slot > 0, block, jnp.zeros_like(block))
        r0, c0 = (at + r * width, c * width) if along_rows else (r * width, at + c * width)
        dense[r0 : r0 + width, c0 : c0 + width] = block


def multiply(n_row, ma, mb, ra_meta, rb_meta, row, a, b, ra, rb, out, left, right):
    width = a.shape[-1]
    depth = BK * width
    for t in range(TICKS):
        if t == 0:
            a_blocks, b_blocks = a, b
            a_place = lambda n: ma[0, n]
            b_place = lambda n: mb[0, n]
        else:
            half = (row[0] + t) // n_row
            a_blocks, b_blocks = ra.at[t - 1], rb.at[t - 1]
            a_place = lambda n, t=t: ra_meta[t - 1, 0, n]
            b_place = lambda n, t=t, half=half: rb_meta[t - 1, half, n]
        fill(left, t * depth, a_blocks, a_place, BR, BK, False)
        fill(right, t * depth, b_blocks, b_place, BK, BC, True)

    tile = 2 * width

    @pl.loop(0, BR * width // tile)
    def _(step):
        rows = pl.ds(pl.multiple_of(step * tile, tile), tile)
        out[rows, :] = jnp.dot(left[rows, :], right[...], preferred_element_type=jnp.float32).astype(out.dtype)


def places(ids, count, numbers):
    slot = jnp.arange(ids.shape[0], dtype=jnp.int32)
    hit = (ids[None, :] == jnp.arange(numbers, dtype=jnp.int32)[:, None]) & (slot < count)[None, :]
    return jnp.sum(jnp.where(hit, slot[None, :] + 1, 0), axis=1)


def shards(n_row, n_col, a_blocks, a_ids, a_count, b_blocks, b_ids, b_count):
    slots = a_blocks.shape[0]
    width = a_blocks.shape[1]
    a_at = places(a_ids[0], a_count[0, 0], BR * BK)
    b_at = jnp.stack(
        [places(b_ids[0, h * slots : (h + 1) * slots], b_count[0, h], BK * BC) for h in range(2)]
    )
    ma = jnp.zeros((8, 128), jnp.int32).at[0, : BR * BK].set(a_at)
    mb = jnp.zeros((8, 128), jnp.int32).at[:2, : BK * BC].set(b_at)
    ra, rb, ra_meta, rb_meta = gather_panels(n_row, n_col, a_blocks, b_blocks, ma, mb)
    row = lax.axis_index("row").astype(jnp.int32).reshape(1)
    smem = pl.BlockSpec(memory_space=pltpu.SMEM)
    depth = TICKS * BK * width

    def whole(count):
        return pl.BlockSpec((count, slots, width, width), lambda g: (0, 0, 0, 0))

    return pl.pallas_call(
        functools.partial(multiply, n_row),
        grid=(1,),
        out_shape=jax.ShapeDtypeStruct((BR * width, BC * width), jnp.bfloat16),
        in_specs=[smem] * 5
        + [
            pl.BlockSpec((slots, width, width), lambda g: (0, 0, 0)),
            pl.BlockSpec((slots, width, width), lambda g: (0, 0, 0)),
            whole(TICKS - 1),
            whole(TICKS - 1),
        ],
        out_specs=pl.BlockSpec((BR * width, BC * width), lambda g: (0, 0)),
        scratch_shapes=[
            pltpu.VMEM((BR * width, depth), jnp.bfloat16),
            pltpu.VMEM((depth, BC * width), jnp.bfloat16),
        ],
        compiler_params=pltpu.CompilerParams(vmem_limit_bytes=48 * 1024 * 1024),
        cost_estimate=pl.CostEstimate(
            flops=2 * BR * width * BC * width * depth, bytes_accessed=10 * 1024 * 1024, transcendentals=0
        ),
    )(ma, mb, ra_meta, rb_meta, row, a_blocks, b_blocks, ra, rb)


def solution(mesh):
    return jax.shard_map(
        functools.partial(shards, mesh.shape["row"], mesh.shape["col"]),
        mesh=mesh,
        in_specs=(
            P("row", "col", None),
            P("row", "col"),
            P("row", "col"),
            P("row", "col", None),
            P("row", "col"),
            P("row", "col"),
        ),
        out_specs=P("row", "col"),
        check_vma=False,
    )
```

time: 387 us -> 97.8 us (0.25)
  the two profiles are of different devices: /device:TPU:248 before, /device:TPU:77 now
where the time goes in v1:
time: 97.8 us; the launch traced here: 97.4 us
  Pallas kernels  88.1 us (90%)
  local copies, waits for them, and re-layouts  6.4 us (7%)
  other arithmetic  2.03 us (2%)
    pallas_call x1, Pallas kernels, gather_panels(): pl.pallas_call(functools.partial(exchange, n_row, n_col), out_shape=[jax....  77.5 us
    pallas_call x1, Pallas kernels, shards(): pl.pallas_call(functools.partial(multiply, n_row), grid=(1,), out_shape=j...  10.6 us
    unnamed x14, local copies, waits for them, and re-layouts  3.09 us

profile of v1, /device:TPU:77, one launch (start us, length us, event | category | flops | bytes accessed | tf_op | source)
XLA Modules:
  0.0 97.4 jit_solution(11475999295887740646)
XLA Ops:
  0.0 0.0 copy-start
  0.0 0.0 copy-start.1
  0.8 0.8 slice_bitcast_fusion
  1.6 1.3 %fusion.3 = (s32[1,1]{1,0:T(1,128)}, s32[1,1]{1,0:T(1,128)}) fusion(s32[1,2]{1,0:T(1,128)} %param.15), kind=kLoop, calls=%fused_computation.16 | loop fusion | bytes 16 | tf_op jit(solution)/shard_map/slice | solution.py:291
  2.9 1.3 %iota_compare_fusion.3 = (pred[24]{0:T(512)(128)(4,1)S(1)}, pred[24]{0:T(512)(128)(4,1)S(1)}) fusion(s32[]{:T(128)} %bitcast.7, s32[]{:T(128)} %bitcast.4), kind=kLoop, calls=%fused_computation.10 | loop fusion | flops 48 | bytes 56 | tf_op jit(solution)/shard_map/lt | solution.py:282
  4.2 0.8 select_reduce_fusion.1
  5.0 0.6 scatter.9.mb
  5.6 0.0 copy-start.3
  5.6 0.6 scatter.6.ma
  6.2 0.0 copy-start.2
  6.2 77.5 %shard_map.64 = (bf16[4,24,128,128]{3,2,1,0:T(8,128)(2,1)}, bf16[3,24,128,128]{3,2,1,0:T(8,128)(2,1)}, s32[3,8,128]{2,1,0:T(8,128)}, s32[3,8,128]{2,1,0:T(8,128)}) custom-call(bf16[24,128,128]{2,1,0:T(8,128)(2,1)} %a.3, bf16[48,128,128]{2,1,0:T(8,128)(2,1)} %b.3, s32[8,128]{1,0:T(8,128)} %scatter.6.ma, s32[8,128]{1,0:T(8,128)} %scatter.9.mb), custom_call_target="tpu_custom_call" | custom-call | tf_op jit(solution)/shard_map/pallas_call | solution.py:223
  83.7 0.0 copy-done
  83.7 0.0 copy-done.1
  83.7 0.0 copy-done.3
  83.7 0.0 copy-done.2
  83.7 0.0 copy-start.4
  83.7 1.7 %copy-done.4 = bf16[3,24,128,128]{3,2,1,0:T(8,128)(2,1)S(1)} copy-done((bf16[3,24,128,128]{3,2,1,0:T(8,128)(2,1)S(1)}, bf16[3,24,128,128]{3,2,1,0:T(8,128)(2,1)}, u32[]{:S(2)}) %copy-start.4) | copy-done | bytes 2359320
  85.4 0.0 copy-start.5
  85.4 0.7 copy-done.5
  86.1 0.0 copy-start.6
  86.1 0.7 copy-done.6
  86.8 10.6 %shard_map.65 = bf16[1024,1024]{1,0:T(8,128)(2,1)} custom-call(s32[8,128]{1,0:T(8,128)S(1)} %copy-done.2, s32[8,128]{1,0:T(8,128)S(1)} %copy-done.3, s32[3,8,128]{2,1,0:T(8,128)S(1)} %copy-done.5, s32[3,8,128]{2,1,0:T(8,128)S(1)} %copy-done.6, s32[1]{0:T(128)} %bitcast.9.row, bf16[24,128,128]{2,1,0:T(8,128)(2,1)S(1)} %copy-done.1, ...), custom_call_target="tpu_custom_call" | custom-call | flops 4294967296 | bytes 10485760 | tf_op jit(solution)/shard_map/pallas_call | solution.py:303
  (3 shorter events, 0.0 us)
Async XLA Ops:
  0.0 83.7 %copy-start = (bf16[48,128,128]{2,1,0:T(8,128)(2,1)S(1)}, bf16[48,128,128]{2,1,0:T(8,128)(2,1)}, u32[]{:S(2)}) copy-start(bf16[48,128,128]{2,1,0:T(8,128)(2,1)} %b.3) | copy-start | bytes 4718596
  0.0 83.7 %copy-start.1 = (bf16[24,128,128]{2,1,0:T(8,128)(2,1)S(1)}, bf16[24,128,128]{2,1,0:T(8,128)(2,1)}, u32[]{:S(2)}) copy-start(bf16[24,128,128]{2,1,0:T(8,128)(2,1)} %a.3) | copy-start | bytes 2359300
  5.6 78.1 %copy-start.3 = (s32[8,128]{1,0:T(8,128)S(1)}, s32[8,128]{1,0:T(8,128)}, u32[]{:S(2)}) copy-start(s32[8,128]{1,0:T(8,128)} %scatter.9.mb) | copy-start | bytes 12292
  6.2 77.5 %copy-start.2 = (s32[8,128]{1,0:T(8,128)S(1)}, s32[8,128]{1,0:T(8,128)}, u32[]{:S(2)}) copy-start(s32[8,128]{1,0:T(8,128)} %scatter.6.ma) | copy-start | bytes 12292
  83.7 1.7 %copy-start.4 = (bf16[3,24,128,128]{3,2,1,0:T(8,128)(2,1)S(1)}, bf16[3,24,128,128]{3,2,1,0:T(8,128)(2,1)}, u32[]{:S(2)}) copy-start(bf16[3,24,128,128]{3,2,1,0:T(8,128)(2,1)} %get-tuple-element.36.rb) | copy-start | bytes 7077892
  85.4 0.7 copy-start.5
  86.1 0.7 copy-start.6

commit v2 on v1

v2 whole, which is shorter than its diff:
```python
import functools

import jax
import jax.numpy as jnp
from jax import lax
from jax.experimental import pallas as pl
from jax.experimental.pallas import tpu as pltpu
from jax.sharding import PartitionSpec as P

BR = 8
BK = 4
BC = 8
TICKS = 4
LANES = 8
MESH = pl.DeviceIdType.MESH


def fill(dense, blocks, place, rows, cols):
    width = blocks.shape[-1]
    for number in range(rows * cols):
        r, c = number // cols, number % cols
        slot = place(number)
        block = blocks[jnp.maximum(slot - 1, 0)]
        block = jnp.where(slot > 0, block, jnp.zeros_like(block))
        dense[r * width : (r + 1) * width, c * width : (c + 1) * width] = block


def kernel(
    n_row, n_col, a, a_ids, a_count, b, b_ids, b_count, out,
    own_a, own_b, ra0, ra1, ra2, ra3, rb0, rb1, rb2, meta, ra_meta, rb_meta, lane_in, lane_mid, lane_out, left, right, total,
    ids_a, count_a, ids_b, count_b, slot_of,
    sem_a, sem_b, sem_m, sem_l, local_sems, meta_sems, send_sems,
):
    ra, rb = (ra0, ra1, ra2, ra3), (rb0, rb1, rb2)
    i, j = lax.axis_index("row"), lax.axis_index("col")
    n_zlo = n_col // 4
    n_z = n_row // LANES * n_zlo
    hop = n_z // 4
    zh, lane = i // LANES, i % LANES
    x, core = lane // 2, lane % 2
    zl, y = j // 4, j % 4
    z = zh * n_zlo + zl
    slots = a.shape[0]
    width = a.shape[-1]
    pieces = 4
    part = slots // pieces
    share = slots // LANES

    locals_ = [
        pltpu.make_async_copy(a_ids, ids_a, local_sems.at[0]),
        pltpu.make_async_copy(a_count, count_a, local_sems.at[1]),
        pltpu.make_async_copy(b_ids, ids_b, local_sems.at[2]),
        pltpu.make_async_copy(b_count, count_b, local_sems.at[3]),
        pltpu.make_async_copy(a, own_a, local_sems.at[4]),
        pltpu.make_async_copy(b.at[pl.ds(0, slots)], own_b, local_sems.at[5]),
    ]
    for copy in locals_:
        copy.start()

    def along_z(steps):
        there = (z + steps + n_z) % n_z
        return ((there // n_zlo) * LANES + lane, (there % n_zlo) * 4 + y)

    barrier = pltpu.get_barrier_semaphore()
    away = hop * (1 - 2 * core)
    senders = [(zh * LANES + (lane + d) % LANES, j) for d in range(1, LANES)]
    senders += [((i + t) % n_row, j) for t in range(1, TICKS)]
    senders += [(i, (j + t) % n_col) for t in range(1, TICKS + 1)]
    senders += [(i, zl * 4 + (y + 1) % 4), (i, zl * 4 + (y + 3) % 4)]
    senders += [along_z(-away)]
    for sender in senders:
        pl.semaphore_signal(barrier, inc=1, device_id=sender, device_id_type=MESH)
    pl.semaphore_wait(barrier, len(senders))

    pending = []

    def send(src, dst, sem, device, slot):
        return pltpu.make_async_remote_copy(
            src_ref=src, dst_ref=dst, send_sem=send_sems.at[slot], recv_sem=sem,
            device_id=device, device_id_type=MESH,
        )

    def start(cond, make):
        slot = len(pending)
        pending.append((cond, functools.partial(make, slot)))
        if cond is None:
            make(slot).start()
        else:
            pl.when(cond)(lambda: make(slot).start())

    def arrived(ref, sem):
        pltpu.make_async_copy(ref, ref, sem).wait()

    def pa(slot, k):
        return ra[slot].at[pl.ds(k * part, part)]

    def pb(slot, k):
        return rb[slot].at[pl.ds(k * part, part)]

    base = slots * (1 - zh)

    @pl.when(lane < 3)
    def _():
        pltpu.make_async_copy(
            b.at[pl.ds(base + share * lane, share)], lane_in.at[lane], sem_l.at[0, lane]
        ).start()

    for d in range(1, LANES):
        to = (lane + d) % LANES
        start(
            lane < 3,
            lambda s, to=to: send(
                b.at[pl.ds(base + share * to, share)], lane_in.at[lane], sem_l.at[0, lane], (zh * LANES + to, j), s
            ),
        )

    up = (y + 2) // 3
    far = (i, (zl - 1 + y // 3 + n_zlo) % n_zlo * 4 + (y + up) % 4)

    def start_far(k):
        mine = a.at[pl.ds(k * part, part)]
        start(y == 0, lambda s: send(mine, pa(3, k), sem_a.at[3, k], far, s))
        start(y > 0, lambda s: send(mine, pa(2, k), sem_a.at[2, k], far, s))

    for k in range(pieces):
        if k < 2:
            start_far(k)
        mine = a.at[pl.ds(k * part, part)]
        start(y > 0, lambda s, k=k, mine=mine: send(mine, pa(0, k), sem_a.at[0, k], (i, j - 1), s))
        own = b.at[pl.ds(k * part, part)]
        start(x > 0, lambda s, k=k, own=own: send(own, pb(1, k), sem_b.at[1, k], (i - 2, j), s))
        start(core == 1, lambda s, k=k, own=own: send(own, pb(0, k), sem_b.at[0, k], (i - 1, j), s))

    for copy in locals_[:4]:
        copy.wait()
    at_row = lax.broadcasted_iota(jnp.int32, meta.shape, 0)
    at_lane = lax.broadcasted_iota(jnp.int32, meta.shape, 1)
    found = jnp.zeros(meta.shape, jnp.int32)
    for s in range(slots):
        name = jnp.where(s < count_a[0, 0], ids_a[0, s], -1)
        found = jnp.where((at_row == 0) & (at_lane == name), s + 1, found)
        for h in range(2):
            name = jnp.where(s < count_b[0, h], ids_b[0, h * slots + s], -1)
            found = jnp.where((at_row == 1 + h) & (at_lane == name), s + 1, found)
    meta[...] = found
    for t in range(1, TICKS):
        start(None, lambda s, t=t: send(meta, ra_meta.at[t - 1], sem_m.at[t - 1], (i, (j - t + n_col) % n_col), s))
        start(None, lambda s, t=t: send(meta, rb_meta.at[t - 1], sem_m.at[t + 2], ((i - t + n_row) % n_row, j), s))
    mine_at = pltpu.make_async_copy(meta, slot_of.at[0], meta_sems.at[0])
    mine_at.start()
    mine_at.wait()
    for copy in locals_[4:]:
        copy.wait()

    tile = 2 * width

    def add_tick(t, a_at, b_at, half, a_panel, b_panel):
        fill(left, a_panel, lambda n: slot_of[a_at, 0, n], BR, BK)
        fill(right, b_panel, lambda n: slot_of[b_at, 1 + half, n], BK, BC)

        @pl.loop(0, BR * width // tile)
        def _(step):
            rows = pl.ds(pl.multiple_of(step * tile, tile), tile)
            product = jnp.dot(left[rows, :], right[...], preferred_element_type=jnp.float32)
            if t > 0:
                product = total[rows, :] + product
            if t < TICKS - 1:
                total[rows, :] = product
            else:
                out[rows, :] = product.astype(out.dtype)

    add_tick(0, 0, 0, 0, own_a, own_b)

    def lanes_first(p):
        arrived(lane_in.at[p], sem_l.at[0, p])
        start(None, lambda s: send(lane_in.at[p], lane_mid.at[p], sem_l.at[1, p], along_z(away), s))

    def lanes_second(p):
        arrived(lane_mid.at[p], sem_l.at[1, p])
        start(None, lambda s: send(lane_mid.at[p], lane_out.at[p], sem_l.at[2, p], along_z(away), s))

    def lanes_last(p):
        arrived(lane_out.at[p], sem_l.at[2, p])
        goal = 6 if p == 0 else 7
        slot = 2 if p == 2 else 1
        into = rb[slot].at[pl.ds(lane * share, share)]
        sem = sem_b.at[slot, lane // 2]

        @pl.when(lane == goal)
        def _():
            pltpu.make_async_copy(lane_out.at[p], into, sem).start()

        start(lane != goal, lambda s: send(lane_out.at[p], into, sem, (zh * LANES + goal, j), s))

    def near(to):
        return (i, zl * 4 + to)

    def forward_first(k):
        low = k < pieces // 2

        @pl.when(y == 0)
        def _():
            arrived(pa(3, k), sem_a.at[3, k])

        start(y == 0, lambda s: send(pa(3, k), pa(2, k), sem_a.at[2, k], near(1), s))
        start(y == 0, lambda s: send(pa(3, k), pa(0, k), sem_a.at[0, k], near(3), s))

        @pl.when((y == 1) | (y == 2))
        def _():
            arrived(pa(0, k), sem_a.at[0, k])

        start(y == 1, lambda s: send(pa(0, k), pa(1, k), sem_a.at[1, k], near(0), s))
        if not low:
            start(y == 2, lambda s: send(pa(0, k), pa(1, k), sem_a.at[1, k], near(1), s))

        @pl.when((y == 0) | (y == 2))
        def _():
            arrived(pa(2, k), sem_a.at[2, k])

        start(y == 2, lambda s: send(pa(2, k), pa(1, k), sem_a.at[1, k], near(3), s))
        if low:
            start(y == 0, lambda s: send(pa(2, k), pa(1, k), sem_a.at[1, k], near(1), s))

    def forward_second(k):
        low = k < pieces // 2

        @pl.when(y == 1)
        def _():
            arrived(pa(2, k), sem_a.at[2, k])

        @pl.when(y == 3)
        def _():
            arrived(pa(0, k), sem_a.at[0, k])

        if low:
            start(y == 1, lambda s: send(pa(2, k), pa(1, k), sem_a.at[1, k], near(2), s))
        else:
            start(y == 3, lambda s: send(pa(0, k), pa(1, k), sem_a.at[1, k], near(2), s))

    def forward_b(k, here):
        @pl.when(here)
        def _():
            arrived(pb(1, k), sem_b.at[1, k])

        start(here & (core == 0), lambda s: send(pb(1, k), pb(0, k), sem_b.at[0, k], (i + 1, j), s))
        start(here & (lane > 0), lambda s: send(pb(1, k), pb(2, k), sem_b.at[2, k], (i - 1, j), s))

    for p in range(3):
        lanes_first(p)
    for k in range(2, pieces):
        start_far(k)
    for k in range(2):
        forward_first(k)
        forward_b(k, x < 3)
    for p in range(3):
        lanes_second(p)
    for k in range(2, pieces):
        forward_first(k)
        forward_b(k, x < 3)
        forward_second(k - 2)
    lanes_last(0)
    forward_second(2)
    lanes_last(1)
    forward_second(3)
    lanes_last(2)
    for k in range(pieces):
        forward_b(k, x == 3)

    for t in range(TICKS - 1):
        arrived(ra_meta.at[t], sem_m.at[t])
        arrived(rb_meta.at[t], sem_m.at[t + 3])
    moves = [pltpu.make_async_copy(ra_meta.at[t], slot_of.at[1 + t], meta_sems.at[1 + t]) for t in range(TICKS - 1)]
    moves += [pltpu.make_async_copy(rb_meta.at[t], slot_of.at[4 + t], meta_sems.at[4 + t]) for t in range(TICKS - 1)]
    for move in moves:
        move.start()
    for move in moves:
        move.wait()
    for t in range(1, TICKS):
        for k in range(pieces):
            if t == 1:
                pl.when(y == 0)(lambda k=k: arrived(pa(0, k), sem_a.at[0, k]))
                arrived(pb(0, k), sem_b.at[0, k])
            if t == 2:
                arrived(pa(1, k), sem_a.at[1, k])
            if t == 3:
                pl.when(y == 3)(lambda k=k: arrived(pa(2, k), sem_a.at[2, k]))
                arrived(pb(2, k), sem_b.at[2, k])
        add_tick(t, t, 3 + t, (i + t) // n_row, ra[t - 1], rb[t - 1])
    for cond, make in pending:
        if cond is None:
            make().wait_send()
        else:
            pl.when(cond)(lambda make=make: make().wait_send())


def shards(n_row, n_col, a_blocks, a_ids, a_count, b_blocks, b_ids, b_count):
    slots = a_blocks.shape[0]
    width = a_blocks.shape[1]
    share = slots // LANES
    kind = a_blocks.dtype
    panel = (slots, width, width)
    hbm = pl.BlockSpec(memory_space=pl.ANY)
    dma = pltpu.SemaphoreType.DMA
    return pl.pallas_call(
        functools.partial(kernel, n_row, n_col),
        out_shape=jax.ShapeDtypeStruct((BR * width, BC * width), kind),
        in_specs=[hbm] * 6,
        out_specs=pl.BlockSpec(memory_space=pltpu.VMEM),
        scratch_shapes=[
            pltpu.VMEM(panel, kind) for _ in range(2 + TICKS + TICKS - 1)
        ]
        + [
            pltpu.VMEM((8, 128), jnp.int32),
            pltpu.VMEM((TICKS - 1, 8, 128), jnp.int32),
            pltpu.VMEM((TICKS - 1, 8, 128), jnp.int32),
        ]
        + [pltpu.VMEM((3, share, width, width), kind)] * 3
        + [
            pltpu.VMEM((BR * width, BK * width), kind),
            pltpu.VMEM((BK * width, BC * width), kind),
            pltpu.VMEM((BR * width, BC * width), jnp.float32),
            pltpu.SMEM(a_ids.shape, jnp.int32),
            pltpu.SMEM(a_count.shape, jnp.int32),
            pltpu.SMEM(b_ids.shape, jnp.int32),
            pltpu.SMEM(b_count.shape, jnp.int32),
            pltpu.SMEM((2 * TICKS - 1, 8, 128), jnp.int32),
            dma((4, 4)), dma((3, 4)), dma((6,)), dma((3, 3)), dma((6,)), dma((7,)), dma((96,)),
        ],
        compiler_params=pltpu.CompilerParams(
            collective_id=0, has_side_effects=True, vmem_limit_bytes=60 * 1024 * 1024
        ),
        cost_estimate=pl.CostEstimate(
            flops=2 * BR * width * BC * width * TICKS * BK * width, bytes_accessed=5 * 1024 * 1024, transcendentals=0
        ),
    )(a_blocks, a_ids, a_count, b_blocks, b_ids, b_count)


def solution(mesh):
    return jax.shard_map(
        functools.partial(shards, mesh.shape["row"], mesh.shape["col"]),
        mesh=mesh,
        in_specs=(
            P("row", "col", None),
            P("row", "col"),
            P("row", "col"),
            P("row", "col", None),
            P("row", "col"),
            P("row", "col"),
        ),
        out_specs=P("row", "col"),
        check_vma=False,
    )
```

time: 97.8 us -> 87.9 us (0.90)
  the two profiles are of different devices: /device:TPU:77 before, /device:TPU:37 now
where the time goes in v2:
time: 87.9 us; the launch traced here: 87.7 us
  Pallas kernels  84 us (96%)
  local copies, waits for them, and re-layouts  3.08 us (4%)
    pallas_call x1, Pallas kernels, shards(): pl.pallas_call(functools.partial(kernel, n_row, n_col), out_shape=jax.Sha...  84 us
    unnamed x1, local copies, waits for them, and re-layouts  3.08 us

profile of v2, /device:TPU:37, one launch (start us, length us, event | category | flops | bytes accessed | tf_op | source)
XLA Modules:
  0.0 87.7 jit_solution(733823974777959728)
XLA Ops:
  0.7 84.0 %shard_map.64 = bf16[1024,1024]{1,0:T(8,128)(2,1)} custom-call(bf16[24,128,128]{2,1,0:T(8,128)(2,1)} %a.1, s32[1,24]{1,0:T(1,128)} %a_ids.1, s32[1,1]{1,0:T(1,128)S(6)} %copy.8.a_count, bf16[48,128,128]{2,1,0:T(8,128)(2,1)} %b.1, s32[1,48]{1,0:T(1,128)} %b_ids.1, s32[1,2]{1,0:T(1,128)} %b_count.1), custom_call_target="tpu_custom_call" | custom-call | flops 4294967296 | bytes 5242880 | tf_op jit(solution)/shard_map/pallas_call | solution.py:304
  84.6 3.1 %copy.9 = bf16[1024,1024]{1,0:T(8,128)(2,1)} copy(bf16[1024,1024]{1,0:T(8,128)(2,1)} %shard_map.64) | data formatting | bytes 4194304

commit v3 on v2

--- a/solution.py
+++ b/solution.py
@@ -27,7 +27,7 @@
 
 def kernel(
     n_row, n_col, a, a_ids, a_count, b, b_ids, b_count, out,
-    own_a, own_b, ra0, ra1, ra2, ra3, rb0, rb1, rb2, meta, ra_meta, rb_meta, lane_in, lane_mid, lane_out, left, right, total,
+    own_a, own_b, ra0, ra1, ra2, ra3, rb0, rb1, rb2, meta, ra_meta, rb_meta, lane_in, lane_mid, lane_out, left0, left1, left2, left3, right, total,
     ids_a, count_a, ids_b, count_b, slot_of,
     sem_a, sem_b, sem_m, sem_l, local_sems, meta_sems, send_sems,
 ):
@@ -70,67 +70,6 @@
     senders += [along_z(-away)]
     for sender in senders:
         pl.semaphore_signal(barrier, inc=1, device_id=sender, device_id_type=MESH)
-    pl.semaphore_wait(barrier, len(senders))
-
-    pending = []
-
-    def send(src, dst, sem, device, slot):
-        return pltpu.make_async_remote_copy(
-            src_ref=src, dst_ref=dst, send_sem=send_sems.at[slot], recv_sem=sem,
-            device_id=device, device_id_type=MESH,
-        )
-
-    def start(cond, make):
-        slot = len(pending)
-        pending.append((cond, functools.partial(make, slot)))
-        if cond is None:
-            make(slot).start()
-        else:
-            pl.when(cond)(lambda: make(slot).start())
-
-    def arrived(ref, sem):
-        pltpu.make_async_copy(ref, ref, sem).wait()
-
-    def pa(slot, k):
-        return ra[slot].at[pl.ds(k * part, part)]
-
-    def pb(slot, k):
-        return rb[slot].at[pl.ds(k * part, part)]
-
-    base = slots * (1 - zh)
-
-    @pl.when(lane < 3)
-    def _():
-        pltpu.make_async_copy(
-            b.at[pl.ds(base + share * lane, share)], lane_in.at[lane], sem_l.at[0, lane]
-        ).start()
-
-    for d in range(1, LANES):
-        to = (lane + d) % LANES
-        start(
-            lane < 3,
-            lambda s, to=to: send(
-                b.at[pl.ds(base + share * to, share)], lane_in.at[lane], sem_l.at[0, lane], (zh * LANES + to, j), s
-            ),
-        )
-
-    up = (y + 2) // 3
-    far = (i, (zl - 1 + y // 3 + n_zlo) % n_zlo * 4 + (y + up) % 4)
-
-    def start_far(k):
-        mine = a.at[pl.ds(k * part, part)]
-        start(y == 0, lambda s: send(mine, pa(3, k), sem_a.at[3, k], far, s))
-        start(y > 0, lambda s: send(mine, pa(2, k), sem_a.at[2, k], far, s))
-
-    for k in range(pieces):
-        if k < 2:
-            start_far(k)
-        mine = a.at[pl.ds(k * part, part)]
-        start(y > 0, lambda s, k=k, mine=mine: send(mine, pa(0, k), sem_a.at[0, k], (i, j - 1), s))
-        own = b.at[pl.ds(k * part, part)]
-        start(x > 0, lambda s, k=k, own=own: send(own, pb(1, k), sem_b.at[1, k], (i - 2, j), s))
-        start(core == 1, lambda s, k=k, own=own: send(own, pb(0, k), sem_b.at[0, k], (i - 1, j), s))
-
     for copy in locals_[:4]:
         copy.wait()
     at_row = lax.broadcasted_iota(jnp.int32, meta.shape, 0)
@@ -143,19 +82,85 @@
             name = jnp.where(s < count_b[0, h], ids_b[0, h * slots + s], -1)
             found = jnp.where((at_row == 1 + h) & (at_lane == name), s + 1, found)
     meta[...] = found
+    mine_at = pltpu.make_async_copy(meta, slot_of.at[0], meta_sems.at[0])
+    mine_at.start()
+    pl.semaphore_wait(barrier, len(senders))
+
+    pending = []
+
+    def send(src, dst, sem, device, slot):
+        return pltpu.make_async_remote_copy(
+            src_ref=src, dst_ref=dst, send_sem=send_sems.at[slot], recv_sem=sem,
+            device_id=device, device_id_type=MESH,
+        )
+
+    def start(cond, make):
+        slot = len(pending)
+        pending.append((cond, functools.partial(make, slot)))
+        if cond is None:
+            make(slot).start()
+        else:
+            pl.when(cond)(lambda: make(slot).start())
+
+    def arrived(ref, sem):
+        pltpu.make_async_copy(ref, ref, sem).wait()
+
+    def pa(slot, k):
+        return ra[slot].at[pl.ds(k * part, part)]
+
+    def pb(slot, k):
+        return rb[slot].at[pl.ds(k * part, part)]
+
+    base = slots * (1 - zh)
+
+    @pl.when(lane < 3)
+    def _():
+        pltpu.make_async_copy(
+            b.at[pl.ds(base + share * lane, share)], lane_in.at[lane], sem_l.at[0, lane]
+        ).start()
+
+    for d in range(1, LANES):
+        to = (lane + d) % LANES
+        start(
+            lane < 3,
+            lambda s, to=to: send(
+                b.at[pl.ds(base + share * to, share)], lane_in.at[lane], sem_l.at[0, lane], (zh * LANES + to, j), s
+            ),
+        )
+
+    up = (y + 2) // 3
+    far = (i, (zl - 1 + y // 3 + n_zlo) % n_zlo * 4 + (y + up) % 4)
+
+    def start_far(k):
+        mine = a.at[pl.ds(k * part, part)]
+        start(y == 0, lambda s: send(mine, pa(3, k), sem_a.at[3, k], far, s))
+        start(y > 0, lambda s: send(mine, pa(2, k), sem_a.at[2, k], far, s))
+
+    for k in range(pieces):
+        if k < 2:
+            start_far(k)
+        mine = a.at[pl.ds(k * part, part)]
+        start(y > 0, lambda s, k=k, mine=mine: send(mine, pa(0, k), sem_a.at[0, k], (i, j - 1), s))
+        own = b.at[pl.ds(k * part, part)]
+        start(x > 0, lambda s, k=k, own=own: send(own, pb(1, k), sem_b.at[1, k], (i - 2, j), s))
+        start(core == 1, lambda s, k=k, own=own: send(own, pb(0, k), sem_b.at[0, k], (i - 1, j), s))
+
     for t in range(1, TICKS):
         start(None, lambda s, t=t: send(meta, ra_meta.at[t - 1], sem_m.at[t - 1], (i, (j - t + n_col) % n_col), s))
         start(None, lambda s, t=t: send(meta, rb_meta.at[t - 1], sem_m.at[t + 2], ((i - t + n_row) % n_row, j), s))
-    mine_at = pltpu.make_async_copy(meta, slot_of.at[0], meta_sems.at[0])
-    mine_at.start()
     mine_at.wait()
     for copy in locals_[4:]:
         copy.wait()
 
     tile = 2 * width
 
-    def add_tick(t, a_at, b_at, half, a_panel, b_panel):
-        fill(left, a_panel, lambda n: slot_of[a_at, 0, n], BR, BK)
+    lefts = (left0, left1, left2, left3)
+
+    def expand_left(t, a_panel):
+        fill(lefts[t], a_panel, lambda n: slot_of[t, 0, n], BR, BK)
+
+    def add_tick(t, b_at, half, b_panel):
+        left = lefts[t]
         fill(right, b_panel, lambda n: slot_of[b_at, 1 + half, n], BK, BC)
 
         @pl.loop(0, BR * width // tile)
@@ -169,7 +174,8 @@
             else:
                 out[rows, :] = product.astype(out.dtype)
 
-    add_tick(0, 0, 0, 0, own_a, own_b)
+    expand_left(0, own_a)
+    add_tick(0, 0, 0, own_b)
 
     def lanes_first(p):
         arrived(lane_in.at[p], sem_l.at[0, p])
@@ -181,16 +187,18 @@
 
     def lanes_last(p):
         arrived(lane_out.at[p], sem_l.at[2, p])
-        goal = 6 if p == 0 else 7
-        slot = 2 if p == 2 else 1
-        into = rb[slot].at[pl.ds(lane * share, share)]
-        sem = sem_b.at[slot, lane // 2]
-
-        @pl.when(lane == goal)
-        def _():
-            pltpu.make_async_copy(lane_out.at[p], into, sem).start()
-
-        start(lane != goal, lambda s: send(lane_out.at[p], into, sem, (zh * LANES + goal, j), s))
+        for goal, slot in (((6, 1), (5, 2)), ((7, 1),), ((7, 2),))[p]:
+            into = rb[slot].at[pl.ds(lane * share, share)]
+            sem = sem_b.at[slot, lane // 2]
+
+            @pl.when(lane == goal)
+            def _():
+                pltpu.make_async_copy(lane_out.at[p], into, sem).start()
+
+            start(
+                lane != goal,
+                lambda s, goal=goal, into=into, sem=sem: send(lane_out.at[p], into, sem, (zh * LANES + goal, j), s),
+            )
 
     def near(to):
         return (i, zl * 4 + to)
@@ -237,13 +245,13 @@
         else:
             start(y == 3, lambda s: send(pa(0, k), pa(1, k), sem_a.at[1, k], near(2), s))
 
-    def forward_b(k, here):
+    def forward_b(k, here, back):
         @pl.when(here)
         def _():
             arrived(pb(1, k), sem_b.at[1, k])
 
         start(here & (core == 0), lambda s: send(pb(1, k), pb(0, k), sem_b.at[0, k], (i + 1, j), s))
-        start(here & (lane > 0), lambda s: send(pb(1, k), pb(2, k), sem_b.at[2, k], (i - 1, j), s))
+        start(back, lambda s: send(pb(1, k), pb(2, k), sem_b.at[2, k], (i - 1, j), s))
 
     for p in range(3):
         lanes_first(p)
@@ -251,20 +259,20 @@
         start_far(k)
     for k in range(2):
         forward_first(k)
-        forward_b(k, x < 3)
+        forward_b(k, x < 3, (x < 3) & (lane > 0))
     for p in range(3):
         lanes_second(p)
     for k in range(2, pieces):
         forward_first(k)
-        forward_b(k, x < 3)
+        forward_b(k, x < 3, (x < 3) & (lane > 0))
         forward_second(k - 2)
+    forward_second(2)
     lanes_last(0)
-    forward_second(2)
+    forward_second(3)
     lanes_last(1)
-    forward_second(3)
     lanes_last(2)
     for k in range(pieces):
-        forward_b(k, x == 3)
+        forward_b(k, x == 3, lane == LANES - 1)
 
     for t in range(TICKS - 1):
         arrived(ra_meta.at[t], sem_m.at[t])
@@ -275,17 +283,17 @@
         move.start()
     for move in moves:
         move.wait()
+    for k in range(pieces):
+        pl.when(y == 0)(lambda k=k: arrived(pa(0, k), sem_a.at[0, k]))
+        pl.when(y == 3)(lambda k=k: arrived(pa(2, k), sem_a.at[2, k]))
+        arrived(pa(1, k), sem_a.at[1, k])
     for t in range(1, TICKS):
-        for k in range(pieces):
-            if t == 1:
-                pl.when(y == 0)(lambda k=k: arrived(pa(0, k), sem_a.at[0, k]))
-                arrived(pb(0, k), sem_b.at[0, k])
-            if t == 2:
-                arrived(pa(1, k), sem_a.at[1, k])
-            if t == 3:
-                pl.when(y == 3)(lambda k=k: arrived(pa(2, k), sem_a.at[2, k]))
-                arrived(pb(2, k), sem_b.at[2, k])
-        add_tick(t, t, 3 + t, (i + t) // n_row, ra[t - 1], rb[t - 1])
+        expand_left(t, ra[t - 1])
+    for t in range(1, TICKS):
+        if t != 2:
+            for k in range(pieces):
+                arrived(pb(t - 1, k), sem_b.at[t - 1, k])
+        add_tick(t, 3 + t, (i + t) // n_row, rb[t - 1])
     for cond, make in pending:
         if cond is None:
             make().wait_send()
@@ -316,7 +324,9 @@
         ]
         + [pltpu.VMEM((3, share, width, width), kind)] * 3
         + [
-            pltpu.VMEM((BR * width, BK * width), kind),
+            pltpu.VMEM((BR * width, BK * width), kind) for _ in range(TICKS)
+        ]
+        + [
             pltpu.VMEM((BK * width, BC * width), kind),
             pltpu.VMEM((BR * width, BC * width), jnp.float32),
             pltpu.SMEM(a_ids.shape, jnp.int32),

time: 87.9 us -> 84.9 us (0.966)
  the two profiles are of different devices: /device:TPU:37 before, /device:TPU:84 now
where the time goes in v3:
time: 84.9 us; the launch traced here: 84.7 us
  Pallas kernels  81 us (95%)
  local copies, waits for them, and re-layouts  3.08 us (4%)
    pallas_call x1, Pallas kernels, shards(): pl.pallas_call(functools.partial(kernel, n_row, n_col), out_shape=jax.Sha...  81 us
    unnamed x1, local copies, waits for them, and re-layouts  3.08 us

profile of v3, /device:TPU:84, one launch (start us, length us, event | category | flops | bytes accessed | tf_op | source)
XLA Modules:
  0.0 84.7 jit_solution(8362696219638301246)
XLA Ops:
  0.7 81.0 %shard_map.64 = bf16[1024,1024]{1,0:T(8,128)(2,1)} custom-call(bf16[24,128,128]{2,1,0:T(8,128)(2,1)} %a.1, s32[1,24]{1,0:T(1,128)} %a_ids.1, s32[1,1]{1,0:T(1,128)S(6)} %copy.8.a_count, bf16[48,128,128]{2,1,0:T(8,128)(2,1)} %b.1, s32[1,48]{1,0:T(1,128)} %b_ids.1, s32[1,2]{1,0:T(1,128)} %b_count.1), custom_call_target="tpu_custom_call" | custom-call | flops 4294967296 | bytes 5242880 | tf_op jit(solution)/shard_map/pallas_call | solution.py:312
  81.6 3.1 %copy.9 = bf16[1024,1024]{1,0:T(8,128)(2,1)} copy(bf16[1024,1024]{1,0:T(8,128)(2,1)} %shard_map.64) | data formatting | bytes 4194304

commit v4 on v3

--- a/solution.py
+++ b/solution.py
@@ -137,8 +137,7 @@
         start(y > 0, lambda s: send(mine, pa(2, k), sem_a.at[2, k], far, s))
 
     for k in range(pieces):
-        if k < 2:
-            start_far(k)
+        start_far(k)
         mine = a.at[pl.ds(k * part, part)]
         start(y > 0, lambda s, k=k, mine=mine: send(mine, pa(0, k), sem_a.at[0, k], (i, j - 1), s))
         own = b.at[pl.ds(k * part, part)]
@@ -255,24 +254,14 @@
 
     for p in range(3):
         lanes_first(p)
-    for k in range(2, pieces):
-        start_far(k)
-    for k in range(2):
+    for k in range(pieces):
         forward_first(k)
         forward_b(k, x < 3, (x < 3) & (lane > 0))
-    for p in range(3):
-        lanes_second(p)
-    for k in range(2, pieces):
-        forward_first(k)
-        forward_b(k, x < 3, (x < 3) & (lane > 0))
-        forward_second(k - 2)
-    forward_second(2)
+        if k > 0:
+            forward_second(k - 1)
+            lanes_second(k - 1)
+    forward_second(pieces - 1)
     lanes_last(0)
-    forward_second(3)
-    lanes_last(1)
-    lanes_last(2)
-    for k in range(pieces):
-        forward_b(k, x == 3, lane == LANES - 1)
 
     for t in range(TICKS - 1):
         arrived(ra_meta.at[t], sem_m.at[t])
@@ -283,17 +272,31 @@
         move.start()
     for move in moves:
         move.wait()
-    for k in range(pieces):
-        pl.when(y == 0)(lambda k=k: arrived(pa(0, k), sem_a.at[0, k]))
-        pl.when(y == 3)(lambda k=k: arrived(pa(2, k), sem_a.at[2, k]))
-        arrived(pa(1, k), sem_a.at[1, k])
-    for t in range(1, TICKS):
-        expand_left(t, ra[t - 1])
-    for t in range(1, TICKS):
+
+    def later_tick(t):
         if t != 2:
             for k in range(pieces):
                 arrived(pb(t - 1, k), sem_b.at[t - 1, k])
         add_tick(t, 3 + t, (i + t) // n_row, rb[t - 1])
+
+    for k in range(pieces):
+        pl.when(y == 0)(lambda k=k: arrived(pa(0, k), sem_a.at[0, k]))
+    expand_left(1, ra[0])
+    pl.when(x < 3)(lambda: later_tick(1))
+    lanes_last(1)
+    for k in range(pieces):
+        arrived(pa(1, k), sem_a.at[1, k])
+    expand_left(2, ra[1])
+    pl.when(x < 3)(lambda: later_tick(2))
+    lanes_last(2)
+    for k in range(pieces):
+        forward_b(k, x == 3, lane == LANES - 1)
+    for k in range(pieces):
+        pl.when(y == 3)(lambda k=k: arrived(pa(2, k), sem_a.at[2, k]))
+    expand_left(3, ra[2])
+    pl.when(x == 3)(lambda: later_tick(1))
+    pl.when(x == 3)(lambda: later_tick(2))
+    later_tick(3)
     for cond, make in pending:
         if cond is None:
             make().wait_send()

time: 84.9 us -> 81.5 us (0.960)
  the two profiles are of different devices: /device:TPU:84 before, /device:TPU:39 now
where the time goes in v4:
time: 81.5 us; the launch traced here: 81.3 us
  Pallas kernels  77.6 us (95%)
  local copies, waits for them, and re-layouts  3.08 us (4%)
    pallas_call x1, Pallas kernels, shards(): pl.pallas_call(functools.partial(kernel, n_row, n_col), out_shape=jax.Sha...  77.6 us
    unnamed x1, local copies, waits for them, and re-layouts  3.08 us

profile of v4, /device:TPU:39, one launch (start us, length us, event | category | flops | bytes accessed | tf_op | source)
XLA Modules:
  0.0 81.3 jit_solution(9781438034289183195)
XLA Ops:
  0.7 77.6 %shard_map.64 = bf16[1024,1024]{1,0:T(8,128)(2,1)} custom-call(bf16[24,128,128]{2,1,0:T(8,128)(2,1)} %a.1, s32[1,24]{1,0:T(1,128)} %a_ids.1, s32[1,1]{1,0:T(1,128)S(6)} %copy.8.a_count, bf16[48,128,128]{2,1,0:T(8,128)(2,1)} %b.1, s32[1,48]{1,0:T(1,128)} %b_ids.1, s32[1,2]{1,0:T(1,128)} %b_count.1), custom_call_target="tpu_custom_call" | custom-call | flops 4294967296 | bytes 5242880 | tf_op jit(solution)/shard_map/pallas_call | solution.py:315
  78.3 3.1 %copy.9 = bf16[1024,1024]{1,0:T(8,128)(2,1)} copy(bf16[1024,1024]{1,0:T(8,128)(2,1)} %shard_map.64) | data formatting | bytes 4194304

commit v5 on v4

--- a/solution.py
+++ b/solution.py
@@ -250,18 +250,22 @@
             arrived(pb(1, k), sem_b.at[1, k])
 
         start(here & (core == 0), lambda s: send(pb(1, k), pb(0, k), sem_b.at[0, k], (i + 1, j), s))
-        start(back, lambda s: send(pb(1, k), pb(2, k), sem_b.at[2, k], (i - 1, j), s))
-
-    for p in range(3):
-        lanes_first(p)
+        if back is not None:
+            start(back, lambda s: send(pb(1, k), pb(2, k), sem_b.at[2, k], (i - 1, j), s))
+
+    lanes_first(0)
     for k in range(pieces):
         forward_first(k)
         forward_b(k, x < 3, (x < 3) & (lane > 0))
         if k > 0:
             forward_second(k - 1)
+        if 0 < k < 3:
             lanes_second(k - 1)
+        if k < 2:
+            lanes_first(k + 1)
+    lanes_last(0)
+    lanes_second(2)
     forward_second(pieces - 1)
-    lanes_last(0)
 
     for t in range(TICKS - 1):
         arrived(ra_meta.at[t], sem_m.at[t])
@@ -282,19 +286,21 @@
     for k in range(pieces):
         pl.when(y == 0)(lambda k=k: arrived(pa(0, k), sem_a.at[0, k]))
     expand_left(1, ra[0])
-    pl.when(x < 3)(lambda: later_tick(1))
+    pl.when(lane < LANES - 1)(lambda: later_tick(1))
     lanes_last(1)
     for k in range(pieces):
         arrived(pa(1, k), sem_a.at[1, k])
     expand_left(2, ra[1])
     pl.when(x < 3)(lambda: later_tick(2))
+    for k in range(pieces):
+        forward_b(k, lane == LANES - 2, None)
     lanes_last(2)
     for k in range(pieces):
-        forward_b(k, x == 3, lane == LANES - 1)
+        forward_b(k, lane == LANES - 1, lane == LANES - 1)
     for k in range(pieces):
         pl.when(y == 3)(lambda k=k: arrived(pa(2, k), sem_a.at[2, k]))
     expand_left(3, ra[2])
-    pl.when(x == 3)(lambda: later_tick(1))
+    pl.when(lane == LANES - 1)(lambda: later_tick(1))
     pl.when(x == 3)(lambda: later_tick(2))
     later_tick(3)
     for cond, make in pending:
@@ -337,7 +343,7 @@
             pltpu.SMEM(b_ids.shape, jnp.int32),
             pltpu.SMEM(b_count.shape, jnp.int32),
             pltpu.SMEM((2 * TICKS - 1, 8, 128), jnp.int32),
-            dma((4, 4)), dma((3, 4)), dma((6,)), dma((3, 3)), dma((6,)), dma((7,)), dma((96,)),
+            dma((4, 4)), dma((3, 4)), dma((6,)), dma((3, 3)), dma((6,)), dma((7,)), dma((112,)),
         ],
         compiler_params=pltpu.CompilerParams(
             collective_id=0, has_side_effects=True, vmem_limit_bytes=60 * 1024 * 1024

time: 81.5 us -> 81.5 us (level)
  the two profiles are of different devices: /device:TPU:39 before, /device:TPU:7 now
where the time goes in v5:
time: 81.5 us; the launch traced here: 80.6 us
  Pallas kernels  76.9 us (94%)
  local copies, waits for them, and re-layouts  3.08 us (4%)
    pallas_call x1, Pallas kernels, shards(): pl.pallas_call(functools.partial(kernel, n_row, n_col), out_shape=jax.Sha...  76.9 us
    unnamed x1, local copies, waits for them, and re-layouts  3.08 us

profile of v5, /device:TPU:7, one launch (start us, length us, event | category | flops | bytes accessed | tf_op | source)
XLA Modules:
  0.0 80.6 jit_solution(16902241091324757283)
XLA Ops:
  0.7 76.9 %shard_map.64 = bf16[1024,1024]{1,0:T(8,128)(2,1)} custom-call(bf16[24,128,128]{2,1,0:T(8,128)(2,1)} %a.1, s32[1,24]{1,0:T(1,128)} %a_ids.1, s32[1,1]{1,0:T(1,128)S(6)} %copy.8.a_count, bf16[48,128,128]{2,1,0:T(8,128)(2,1)} %b.1, s32[1,48]{1,0:T(1,128)} %b_ids.1, s32[1,2]{1,0:T(1,128)} %b_count.1), custom_call_target="tpu_custom_call" | custom-call | flops 4294967296 | bytes 5242880 | tf_op jit(solution)/shard_map/pallas_call | solution.py:321
  77.6 3.1 %copy.9 = bf16[1024,1024]{1,0:T(8,128)(2,1)} copy(bf16[1024,1024]{1,0:T(8,128)(2,1)} %shard_map.64) | data formatting | bytes 4194304

commit v6 on v5

--- a/solution.py
+++ b/solution.py
@@ -70,6 +70,66 @@
     senders += [along_z(-away)]
     for sender in senders:
         pl.semaphore_signal(barrier, inc=1, device_id=sender, device_id_type=MESH)
+    pl.semaphore_wait(barrier, len(senders))
+
+    pending = []
+
+    def send(src, dst, sem, device, slot):
+        return pltpu.make_async_remote_copy(
+            src_ref=src, dst_ref=dst, send_sem=send_sems.at[slot], recv_sem=sem,
+            device_id=device, device_id_type=MESH,
+        )
+
+    def start(cond, make):
+        slot = len(pending)
+        pending.append((cond, functools.partial(make, slot)))
+        if cond is None:
+            make(slot).start()
+        else:
+            pl.when(cond)(lambda: make(slot).start())
+
+    def arrived(ref, sem):
+        pltpu.make_async_copy(ref, ref, sem).wait()
+
+    def pa(slot, k):
+        return ra[slot].at[pl.ds(k * part, part)]
+
+    def pb(slot, k):
+        return rb[slot].at[pl.ds(k * part, part)]
+
+    base = slots * (1 - zh)
+
+    @pl.when(lane < 3)
+    def _():
+        pltpu.make_async_copy(
+            b.at[pl.ds(base + share * lane, share)], lane_in.at[lane], sem_l.at[0, lane]
+        ).start()
+
+    for d in range(1, LANES):
+        to = (lane + d) % LANES
+        start(
+            lane < 3,
+            lambda s, to=to: send(
+                b.at[pl.ds(base + share * to, share)], lane_in.at[lane], sem_l.at[0, lane], (zh * LANES + to, j), s
+            ),
+        )
+
+    up = (y + 2) // 3
+    far = (i, (zl - 1 + y // 3 + n_zlo) % n_zlo * 4 + (y + up) % 4)
+
+    def start_far(k):
+        mine = a.at[pl.ds(k * part, part)]
+        start(y == 0, lambda s: send(mine, pa(3, k), sem_a.at[3, k], far, s))
+        start(y > 0, lambda s: send(mine, pa(2, k), sem_a.at[2, k], far, s))
+
+    for k in range(pieces):
+        start_far(k)
+        mine = a.at[pl.ds(k * part, part)]
+        start(y > 0, lambda s, k=k, mine=mine: send(mine, pa(0, k), sem_a.at[0, k], (i, j - 1), s))
+        own = b.at[pl.ds(k * part, part)]
+        start(x > 0, lambda s, k=k, own=own: send(own, pb(1, k), sem_b.at[1, k], (i - 2, j), s))
+        start(core == 1, lambda s, k=k, own=own: send(own, pb(0, k), sem_b.at[0, k], (i - 1, j), s))
+
     for copy in locals_[:4]:
         copy.wait()
     at_row = lax.broadcasted_iota(jnp.int32, meta.shape, 0)
@@ -84,72 +144,9 @@
     meta[...] = found
     mine_at = pltpu.make_async_copy(meta, slot_of.at[0], meta_sems.at[0])
     mine_at.start()
-    pl.semaphore_wait(barrier, len(senders))
-
-    pending = []
-
-    def send(src, dst, sem, device, slot):
-        return pltpu.make_async_remote_copy(
-            src_ref=src, dst_ref=dst, send_sem=send_sems.at[slot], recv_sem=sem,
-            device_id=device, device_id_type=MESH,
-        )
-
-    def start(cond, make):
-        slot = len(pending)
-        pending.append((cond, functools.partial(make, slot)))
-        if cond is None:
-            make(slot).start()
-        else:
-            pl.when(cond)(lambda: make(slot).start())
-
-    def arrived(ref, sem):
-        pltpu.make_async_copy(ref, ref, sem).wait()
-
-    def pa(slot, k):
-        return ra[slot].at[pl.ds(k * part, part)]
-
-    def pb(slot, k):
-        return rb[slot].at[pl.ds(k * part, part)]
-
-    base = slots * (1 - zh)
-
-    @pl.when(lane < 3)
-    def _():
-        pltpu.make_async_copy(
-            b.at[pl.ds(base + share * lane, share)], lane_in.at[lane], sem_l.at[0, lane]
-        ).start()
-
-    for d in range(1, LANES):
-        to = (lane + d) % LANES
-        start(
-            lane < 3,
-            lambda s, to=to: send(
-                b.at[pl.ds(base + share * to, share)], lane_in.at[lane], sem_l.at[0, lane], (zh * LANES + to, j), s
-            ),
-        )
-
-    up = (y + 2) // 3
-    far = (i, (zl - 1 + y // 3 + n_zlo) % n_zlo * 4 + (y + up) % 4)
-
-    def start_far(k):
-        mine = a.at[pl.ds(k * part, part)]
-        start(y == 0, lambda s: send(mine, pa(3, k), sem_a.at[3, k], far, s))
-        start(y > 0, lambda s: send(mine, pa(2, k), sem_a.at[2, k], far, s))
-
-    for k in range(pieces):
-        start_far(k)
-        mine = a.at[pl.ds(k * part, part)]
-        start(y > 0, lambda s, k=k, mine=mine: send(mine, pa(0, k), sem_a.at[0, k], (i, j - 1), s))
-        own = b.at[pl.ds(k * part, part)]
-        start(x > 0, lambda s, k=k, own=own: send(own, pb(1, k), sem_b.at[1, k], (i - 2, j), s))
-        start(core == 1, lambda s, k=k, own=own: send(own, pb(0, k), sem_b.at[0, k], (i - 1, j), s))
-
     for t in range(1, TICKS):
         start(None, lambda s, t=t: send(meta, ra_meta.at[t - 1], sem_m.at[t - 1], (i, (j - t + n_col) % n_col), s))
         start(None, lambda s, t=t: send(meta, rb_meta.at[t - 1], sem_m.at[t + 2], ((i - t + n_row) % n_row, j), s))
-    mine_at.wait()
-    for copy in locals_[4:]:
-        copy.wait()
 
     tile = 2 * width
 
@@ -173,8 +170,12 @@
             else:
                 out[rows, :] = product.astype(out.dtype)
 
-    expand_left(0, own_a)
-    add_tick(0, 0, 0, own_b)
+    def first_tick():
+        mine_at.wait()
+        for copy in locals_[4:]:
+            copy.wait()
+        expand_left(0, own_a)
+        add_tick(0, 0, 0, own_b)
 
     def lanes_first(p):
         arrived(lane_in.at[p], sem_l.at[0, p])
@@ -263,6 +264,8 @@
             lanes_second(k - 1)
         if k < 2:
             lanes_first(k + 1)
+        if k == 1:
+            first_tick()
     lanes_last(0)
     lanes_second(2)
     forward_second(pieces - 1)
@@ -294,14 +297,19 @@
     pl.when(x < 3)(lambda: later_tick(2))
     for k in range(pieces):
         forward_b(k, lane == LANES - 2, None)
+    for k in range(pieces):
+        forward_b(k, lane == LANES - 1, lane == LANES - 1)
+
+    @pl.when(lane == LANES - 1)
+    def _():
+        later_tick(1)
+        later_tick(2)
+
     lanes_last(2)
-    for k in range(pieces):
-        forward_b(k, lane == LANES - 1, lane == LANES - 1)
     for k in range(pieces):
         pl.when(y == 3)(lambda k=k: arrived(pa(2, k), sem_a.at[2, k]))
     expand_left(3, ra[2])
-    pl.when(lane == LANES - 1)(lambda: later_tick(1))
-    pl.when(x == 3)(lambda: later_tick(2))
+    pl.when(lane == LANES - 2)(lambda: later_tick(2))
     later_tick(3)
     for cond, make in pending:
         if cond is None:

time: 81.5 us -> 84.2 us (1.033)
  Pallas kernels: 76.9 us -> 80.2 us
    pallas_call x1, Pallas kernels: 76.9 us -> 80.2 us  [shards(): pl.pallas_call(functools.partial(kernel, n_row, n_col), out_shape=jax.Sha...]
where the time goes in v6:
time: 84.2 us; the launch traced here: 84 us
  Pallas kernels  80.2 us (95%)
  local copies, waits for them, and re-layouts  3.08 us (4%)
    pallas_call x1, Pallas kernels, shards(): pl.pallas_call(functools.partial(kernel, n_row, n_col), out_shape=jax.Sha...  80.2 us
    unnamed x1, local copies, waits for them, and re-layouts  3.08 us

profile of v6, /device:TPU:7, one launch (start us, length us, event | category | flops | bytes accessed | tf_op | source)
XLA Modules:
  0.0 84.0 jit_solution(97135735791335495)
XLA Ops:
  0.7 80.2 %shard_map.64 = bf16[1024,1024]{1,0:T(8,128)(2,1)} custom-call(bf16[24,128,128]{2,1,0:T(8,128)(2,1)} %a.1, s32[1,24]{1,0:T(1,128)} %a_ids.1, s32[1,1]{1,0:T(1,128)S(6)} %copy.8.a_count, bf16[48,128,128]{2,1,0:T(8,128)(2,1)} %b.1, s32[1,48]{1,0:T(1,128)} %b_ids.1, s32[1,2]{1,0:T(1,128)} %b_count.1), custom_call_target="tpu_custom_call" | custom-call | flops 4294967296 | bytes 5242880 | tf_op jit(solution)/shard_map/pallas_call | solution.py:329
  80.9 3.1 %copy.9 = bf16[1024,1024]{1,0:T(8,128)(2,1)} copy(bf16[1024,1024]{1,0:T(8,128)(2,1)} %shard_map.64) | data formatting | bytes 4194304

commit v7 on v5

--- a/solution.py
+++ b/solution.py
@@ -137,7 +137,8 @@
         start(y > 0, lambda s: send(mine, pa(2, k), sem_a.at[2, k], far, s))
 
     for k in range(pieces):
-        start_far(k)
+        if k < 2:
+            start_far(k)
         mine = a.at[pl.ds(k * part, part)]
         start(y > 0, lambda s, k=k, mine=mine: send(mine, pa(0, k), sem_a.at[0, k], (i, j - 1), s))
         own = b.at[pl.ds(k * part, part)]
@@ -263,6 +264,7 @@
             lanes_second(k - 1)
         if k < 2:
             lanes_first(k + 1)
+            start_far(k + 2)
     lanes_last(0)
     lanes_second(2)
     forward_second(pieces - 1)

time: 81.5 us -> 85.8 us (1.053)
  the two profiles are of different devices: /device:TPU:7 before, /device:TPU:47 now
where the time goes in v7:
time: 85.8 us; the launch traced here: 85.7 us
  Pallas kernels  81.9 us (95%)
  local copies, waits for them, and re-layouts  3.08 us (4%)
    pallas_call x1, Pallas kernels, shards(): pl.pallas_call(functools.partial(kernel, n_row, n_col), out_shape=jax.Sha...  81.9 us
    unnamed x1, local copies, waits for them, and re-layouts  3.08 us

profile of v7, /device:TPU:47, one launch (start us, length us, event | category | flops | bytes accessed | tf_op | source)
XLA Modules:
  0.0 85.7 jit_solution(16875686790522506283)
XLA Ops:
  0.7 81.9 %shard_map.64 = bf16[1024,1024]{1,0:T(8,128)(2,1)} custom-call(bf16[24,128,128]{2,1,0:T(8,128)(2,1)} %a.1, s32[1,24]{1,0:T(1,128)} %a_ids.1, s32[1,1]{1,0:T(1,128)S(6)} %copy.8.a_count, bf16[48,128,128]{2,1,0:T(8,128)(2,1)} %b.1, s32[1,48]{1,0:T(1,128)} %b_ids.1, s32[1,2]{1,0:T(1,128)} %b_count.1), custom_call_target="tpu_custom_call" | custom-call | flops 4294967296 | bytes 5242880 | tf_op jit(solution)/shard_map/pallas_call | solution.py:323
  82.6 3.1 %copy.9 = bf16[1024,1024]{1,0:T(8,128)(2,1)} copy(bf16[1024,1024]{1,0:T(8,128)(2,1)} %shard_map.64) | data formatting | bytes 4194304

commit v8 on v5

--- a/solution.py
+++ b/solution.py
@@ -263,8 +263,8 @@
             lanes_second(k - 1)
         if k < 2:
             lanes_first(k + 1)
+    lanes_second(2)
     lanes_last(0)
-    lanes_second(2)
     forward_second(pieces - 1)
 
     for t in range(TICKS - 1):

time: 81.5 us -> 81.5 us (level)
  no operation moved by 1% of the time
where the time goes in v8:
time: 81.5 us; the launch traced here: 80.7 us
  Pallas kernels  76.9 us (94%)
  local copies, waits for them, and re-layouts  3.08 us (4%)
    pallas_call x1, Pallas kernels, shards(): pl.pallas_call(functools.partial(kernel, n_row, n_col), out_shape=jax.Sha...  76.9 us
    unnamed x1, local copies, waits for them, and re-layouts  3.08 us

profile of v8, /device:TPU:7, one launch (start us, length us, event | category | flops | bytes accessed | tf_op | source)
XLA Modules:
  0.0 80.7 jit_solution(2586338875061808781)
XLA Ops:
  0.7 76.9 %shard_map.64 = bf16[1024,1024]{1,0:T(8,128)(2,1)} custom-call(bf16[24,128,128]{2,1,0:T(8,128)(2,1)} %a.1, s32[1,24]{1,0:T(1,128)} %a_ids.1, s32[1,1]{1,0:T(1,128)S(6)} %copy.8.a_count, bf16[48,128,128]{2,1,0:T(8,128)(2,1)} %b.1, s32[1,48]{1,0:T(1,128)} %b_ids.1, s32[1,2]{1,0:T(1,128)} %b_count.1), custom_call_target="tpu_custom_call" | custom-call | flops 4294967296 | bytes 5242880 | tf_op jit(solution)/shard_map/pallas_call | solution.py:321
  77.6 3.1 %copy.9 = bf16[1024,1024]{1,0:T(8,128)(2,1)} copy(bf16[1024,1024]{1,0:T(8,128)(2,1)} %shard_map.64) | data formatting | bytes 4194304
